TPU v7x, 32 devices: a whole 2x2x4 slice. The times are simulated.
32 devices in a mesh: grp: 2 (over y), row: 4 (over x, core), col: 4 (over z).
Axes of the slice: x: 2, y: 2, z: 4, core: 2. Of those that a mesh axis runs over, the one named last changes fastest.
Arguments:
- probes: float32 [64, 16, 256], P(('grp', 'row', 'col')), parts along dimension 0, may hold values from -48 to 48, as said below
- mass: float32 [64, 256], P(('grp', 'row', 'col')), parts along dimension 0, may hold values from 1.05 to 2.5
- blocks: bfloat16 [8, 4, 14, 256, 256], P(('grp', 'row'), 'col'), parts along dimension 0, may hold values from -0.00029945374 to 0
- slot_rows: int32 [8, 4, 14], P(('grp', 'row'), 'col'), parts along dimension 0, may hold values from 0 to 7, as said below
- slot_cols: int32 [8, 4, 14], P(('grp', 'row'), 'col'), parts along dimension 0, may hold values from 0 to 7, as said below
- slot_count: int32 [8, 4], P(('grp', 'row'), 'col'), parts along dimension 0, may hold values from 1 to 14, as said below
Outputs:
- solution_field: float32 [64, 16, 256], P(('grp', 'row', 'col')), parts along dimension 0
- residual: float32 [64, 16, 256], P(('grp', 'row', 'col')), parts along dimension 0
There are 2 independent parts, one for each index of `grp`. A program takes and returns all parts, laid end to end along the dimension named above; each array names one. Nothing has to cross between parts.
Inputs may be any that keep to these rules, and one draw needn't show every extreme that they name: `probes`: probes are finite. `slot_rows`: block pairs follow a banded lattice pattern with block offsets 0, 1, 2, 3, 4, 5 and 8; every diagonal block is stored; other blocks of the band may be missing. Padding slots hold 0. `slot_cols`: padding slots hold 0. `slot_count`: some device has all 14 slots live.
All inputs are finite; a program needn't handle non-finite values.
Results may differ from a plain program's by a relative error of at most 0.0003.
Values may be sent and summed in bfloat16 or wider, within the bound.
A program may use at most 64 MiB of HBM per device.

v0:
```python
import jax
import jax.numpy as jnp
from jax import lax
from jax.sharding import PartitionSpec as P

ITERS = 2


def shifted(value, axis, steps):
    count = lax.axis_size(axis)
    initial, last = (max(0, -steps), min(count, count - steps))
    return lax.ppermute(value, axis, [(source, source + steps) for source in range(initial, last)])


def gram(first, second):
    return jnp.einsum("ipk,iqk->pq", first, second, precision=lax.Precision.HIGHEST)


def solve_sym(matrix, right):
    sym = 0.5 * (matrix + matrix.T)
    factor = jnp.linalg.cholesky(sym)
    inner = lax.linalg.triangular_solve(factor, right, left_side=True, lower=True)
    return lax.linalg.triangular_solve(factor, inner, left_side=True, lower=True, transpose_a=True)


def mix(field, coef):
    return jnp.einsum("ipk,pq->iqk", field, coef, precision=lax.Precision.HIGHEST)


def position_of(values, choices_list):
    found = jnp.zeros(values.shape, jnp.int32)
    for place, value in enumerate(choices_list):
        found = found + jnp.where(values == value, place, 0).astype(jnp.int32)
    return found


def shards(probes, mass, blocks, slot_rows, slot_cols, slot_count):
    vec_blocks = probes.shape[0]
    width = probes.shape[1]
    nodes = probes.shape[2]
    count_col = lax.axis_size("col")
    count_row = lax.axis_size("row")
    nbr = vec_blocks * count_col
    row_at = lax.axis_index("row")
    col_at = lax.axis_index("col")
    tiles = blocks[0, 0]
    lrows = slot_rows[0, 0]
    lcols = slot_cols[0, 0]
    live_count = slot_count[0, 0]
    slots = tiles.shape[0]
    grow = row_at * nbr + lrows
    gcol = (lcols // vec_blocks * count_col + col_at) * vec_blocks + lcols % vec_blocks
    upper = jnp.arange(nodes)[:, None] < jnp.arange(nodes)[None, :]
    keep = jnp.where((grow == gcol)[:, None, None], upper[None, :, :], True).astype(jnp.bfloat16)
    tiles = tiles * keep
    live = jnp.arange(slots, dtype=jnp.int32) < live_count
    targets = jnp.arange(nbr, dtype=jnp.int32)[:, None]
    row_hot = ((lrows[None, :] == targets) & live[None, :]).astype(jnp.float32)
    total_blocks = vec_blocks * count_col * count_row
    plane = total_blocks // 8
    offsets = [0, 1, 2, plane - 1, plane, plane + 1, 2 * plane]
    deltas = sorted(
        set(
            [o // vec_blocks for o in offsets]
            + [(o + vec_blocks - 1) // vec_blocks for o in offsets]
        )
    )
    row_dists = sorted(
        set(
            [
                (first + d) // count_col
                for first in range(count_col)
                for d in deltas
                if (first + d) // count_col < count_row
            ]
        )
    )
    local_rows = jnp.arange(vec_blocks, dtype=jnp.int32)[:, None]
    col_pos = position_of(lcols // vec_blocks - row_at, row_dists)
    solution_field = jnp.zeros_like(probes)
    residual = probes
    direction = probes
    norm_now = lax.psum(gram(residual, residual), ("row", "col"))
    for step in range(ITERS):
        apply_low = direction.astype(jnp.bfloat16)
        col_pieces = []
        for near_dist in row_dists:
            if near_dist == 0:
                col_pieces.append(apply_low)
            else:
                col_pieces.append(shifted(apply_low, "row", -near_dist))
        col_stack = jnp.stack(col_pieces, 0)
        col_slot = col_stack[col_pos, lcols % vec_blocks]
        forward = jnp.einsum(
            "spk,sjk->spj", col_slot, tiles, preferred_element_type=jnp.float32
        ).reshape(slots, width * nodes)
        row_vec = lax.all_gather(apply_low, "col", axis=0, tiled=True)
        apply_backward = jnp.einsum(
            "spj,sjk->spk", row_vec[lrows], tiles, preferred_element_type=jnp.float32
        ).reshape(slots, width * nodes)
        row_part = jnp.dot(row_hot, forward, precision=lax.Precision.HIGHEST).reshape(
            nbr, width, nodes
        )
        row_total = lax.psum_scatter(
            row_part.astype(jnp.bfloat16), "col", scatter_dimension=0, tiled=True
        ).astype(jnp.float32)
        col_total = jnp.zeros((vec_blocks, width, nodes), jnp.float32)
        for dist in row_dists:
            owner = row_at + dist
            hot = ((lcols[None, :] == owner * vec_blocks + local_rows) & live[None, :]).astype(
                jnp.float32
            )
            part_sum = jnp.dot(hot, apply_backward, precision=lax.Precision.HIGHEST).reshape(
                vec_blocks, width, nodes
            )
            if dist == 0:
                col_total = col_total + part_sum
            else:
                col_total = col_total + shifted(part_sum.astype(jnp.bfloat16), "row", dist).astype(
                    part_sum.dtype
                )
        image = row_total + col_total + mass[:, None, :] * direction
        more = step + 1 < ITERS
        curv = lax.psum(gram(direction, image), ("row", "col"))
        alpha = solve_sym(curv, norm_now)
        solution_field = solution_field + mix(direction, alpha)
        residual = residual - mix(image, alpha)
        if more:
            norm_next = lax.psum(gram(residual, residual), ("row", "col"))
        if more:
            beta = solve_sym(norm_now, norm_next)
            direction = residual + mix(direction, beta)
            norm_now = norm_next
    return (solution_field, residual)


def solution(mesh):
    placed = (
        P(("grp", "row", "col"), None, None),
        P(("grp", "row", "col"), None),
        P(("grp", "row"), "col", None, None, None),
        P(("grp", "row"), "col", None),
        P(("grp", "row"), "col", None),
        P(("grp", "row"), "col"),
    )
    return jax.shard_map(
        shards,
        mesh=mesh,
        in_specs=placed,
        out_specs=(P(("grp", "row", "col"), None, None), P(("grp", "row", "col"), None, None)),
        check_vma=False,
    )
```

profile of v0, /device:TPU:0, one launch (start us, length us, event | category | flops | bytes accessed | tf_op | source)
XLA Modules:
  0.0 240.0 jit_solution(11736569097378006783)
XLA Ops:
  7.2 0.8 convert_element_type.36
  8.0 1.3 collective-permute-start
  9.3 14.9 %all_gather.6 = bf16[8,16,256]{2,1,0:T(8,128)(2,1)S(1)} all-gather(bf16[2,16,256]{2,1,0:T(8,128)(2,1)S(1)} %convert_element_type.36), channel_id=1, replica_groups=mesh['grp'=2,'row'=4,'col'=4] {'col'}, dimensions={0}, use_global_device_ids=true | all-gather | bytes 81920 | tf_op jit(solution)/shard_map/all_gather | solution.py:97
  24.2 0.7 fusion.65
  24.8 0.6 gather_fusion.1
  25.4 0.7 fusion.59
  26.1 2.0 select_select_fusion
  28.1 0.3 fusion.77
  29.2 0.3 fusion.8
  29.6 1.3 collective-permute-start.1
  31.0 0.6 gather_fusion
  31.6 0.6 fusion.76
  32.2 0.3 convolution_convert_fusion.1
  32.5 0.6 copy.107
  33.3 0.3 fusion.10
  33.6 0.1 convolution_bitcast_fusion.8
  33.8 21.2 %reduce-scatter.3.cloned.1.call-done = bf16[2,16,256]{2,1,0:T(8,128)(2,1)} async-done(((bf16[8,16,256]{2,1,0:T(8,128)(2,1)}), bf16[2,16,256]{2,1,0:T(8,128)(2,1)}) %reduce-scatter.3.cloned.1.call-update) | async-done | bytes 16400 | tf_op jit(solution)/shard_map/reduce_scatter | solution.py:104
  54.9 0.9 convolution_bitcast_fusion.9
  55.8 57.9 %all-reduce = (f32[16,16]{1,0:T(8,128)S(1)}, f32[16,16]{1,0:T(8,128)S(1)}) all-reduce(f32[16,16]{1,0:T(8,128)S(1)} %convolution_bitcast_fusion.8, f32[16,16]{1,0:T(8,128)S(1)} %convolution_bitcast_fusion.9), channel_id=1, replica_groups=mesh['grp'=2,'row'=4,'col'=4] {'row','col'}, use_global_device_ids=true, to_apply=%region_4.6 | all-reduce | flops 512 | bytes 4096 | tf_op jit(solution)/shard_map/psum | solution.py:83
  113.7 0.1 copy.117
  113.8 0.1 copy.113
  113.9 0.1 copy.118
  114.0 1.5 cholesky.70
  115.5 0.6 compare_reduce_fusion.1
  116.1 0.6 fusion.23
  116.8 1.2 custom-call.19
  118.0 0.1 copy.114
  118.1 1.5 cholesky.59
  119.6 0.6 compare_reduce_fusion.2
  120.2 0.6 fusion.22
  120.9 1.2 custom-call.17
  122.1 0.2 fusion.35
  122.3 0.2 convolution_bitcast_fusion.7
  122.5 0.9 fusion.3
  123.4 0.1 convolution_bitcast_fusion.6
  123.6 30.7 %psum.30 = f32[16,16]{1,0:T(8,128)S(1)} all-reduce(f32[16,16]{1,0:T(8,128)S(1)} %convolution_bitcast_fusion.6), channel_id=1, replica_groups=mesh['grp'=2,'row'=4,'col'=4] {'row','col'}, use_global_device_ids=true, to_apply=%region_5.9 | all-reduce | flops 256 | bytes 2048 | tf_op jit(solution)/shard_map/psum | solution.py:129
  154.3 0.2 fusion.30
  154.5 0.2 convolution_bitcast_fusion.5
  154.7 0.2 fusion.75
  154.9 1.3 collective-permute-start.2
  156.2 13.1 %all_gather.7 = bf16[8,16,256]{2,1,0:T(8,128)(2,1)S(1)} all-gather(bf16[2,16,256]{2,1,0:T(8,128)(2,1)S(1)} %get-tuple-element.13), channel_id=1, replica_groups=mesh['grp'=2,'row'=4,'col'=4] {'col'}, dimensions={0}, use_global_device_ids=true | all-gather | bytes 81920 | tf_op jit(solution)/shard_map/all_gather | solution.py:97
  169.3 0.6 gather_fusion.3
  169.9 0.4 fusion.80
  170.2 0.3 fusion.6
  170.6 0.3 fusion.4
  170.9 1.3 collective-permute-start.3
  172.3 0.6 gather_fusion.2
  172.9 0.6 fusion.79
  173.5 0.3 convolution_convert_fusion
  173.8 0.6 copy.121
  174.5 0.1 fusion.78
  174.7 20.1 %reduce-scatter.5.cloned.1.call-done = bf16[2,16,256]{2,1,0:T(8,128)(2,1)} async-done(((bf16[8,16,256]{2,1,0:T(8,128)(2,1)}), bf16[2,16,256]{2,1,0:T(8,128)(2,1)}) %reduce-scatter.5.cloned.1.call-update) | async-done | bytes 16400 | tf_op jit(solution)/shard_map/reduce_scatter | solution.py:104
  194.8 0.9 convolution_bitcast_fusion.4
  195.6 30.7 %psum.31 = f32[16,16]{1,0:T(8,128)S(1)} all-reduce(f32[16,16]{1,0:T(8,128)S(1)} %convolution_bitcast_fusion.4), channel_id=1, replica_groups=mesh['grp'=2,'row'=4,'col'=4] {'row','col'}, use_global_device_ids=true, to_apply=%region_7.11 | all-reduce | flops 256 | bytes 2048 | tf_op jit(solution)/shard_map/psum | solution.py:124
  226.3 0.1 copy.126
  226.4 0.1 copy.127
  226.5 1.5 cholesky.81
  228.0 0.6 compare_reduce_fusion
  228.6 0.6 fusion.24
  229.3 1.2 custom-call.21
  230.5 0.2 fusion.25
  230.7 0.2 convolution_bitcast_fusion.3
  230.9 0.8 fusion.1
  231.7 1.5 fusion
  (39 shorter events, 0.5 us)
Async XLA Ops:
  7.2 47.8 %reduce-scatter.3.cloned.1.call-start = ((), (), s32[]{:S(2)}) async-start(), calls=%async_computation.2 | async-start | bytes 81920 | tf_op jit(solution)/shard_map/reduce_scatter | solution.py:104
  8.0 22.9 %collective-permute-start = (bf16[2,16,256]{2,1,0:T(8,128)(2,1)S(1)}, bf16[2,16,256]{2,1,0:T(8,128)(2,1)S(1)}, u32[]{:S(2)}, u32[]{:S(2)}) collective-permute-start(bf16[2,16,256]{2,1,0:T(8,128)(2,1)S(1)} %convert_element_type.36), channel_id=1, source_target_pairs={{4,0},{8,4},{12,8},{5,1},{9,5},{13,9},{6,2},{10,6},{14,10},{7,3},{... | collective-permute-start | bytes 49160 | tf_op jit(solution)/shard_map/ppermute | solution.py:12
  28.1 1.1 copy-start.2
  28.1 2.8 %copy-start = (f32[2,16,256]{2,1,0:T(8,128)S(1)}, f32[2,16,256]{2,1,0:T(8,128)}, u32[]{:S(2)}) copy-start(f32[2,16,256]{2,1,0:T(8,128)} %param.11) | copy-start | bytes 98308
  28.5 3.7 %copy-start.3 = (s32[1,1,14]{2,1,0:T(1,128)S(1)}, s32[1,1,14]{2,1,0:T(1,128)}, u32[]{:S(2)}) copy-start(s32[1,1,14]{2,1,0:T(1,128)} %param.14) | copy-start | bytes 172
  29.6 4.2 %collective-permute-start.1 = (bf16[2,16,256]{2,1,0:T(8,128)(2,1)S(1)}, bf16[2,16,256]{2,1,0:T(8,128)(2,1)S(1)}, u32[]{:S(2)}, u32[]{:S(2)}) collective-permute-start(bf16[2,16,256]{2,1,0:T(8,128)(2,1)S(1)} %copy.172), channel_id=1, source_target_pairs={{0,4},{4,8},{8,12},{1,5},{5,9},{9,13},{2,6},{6,10},{10,14},{3,7},{... | collective-permute-start | bytes 49160 | tf_op jit(solution)/shard_map/ppermute | solution.py:12
  30.9 24.0 %copy-start.1 = (f32[2,256]{1,0:T(2,128)S(1)}, f32[2,256]{1,0:T(2,128)}, u32[]{:S(2)}) copy-start(f32[2,256]{1,0:T(2,128)} %param.12) | copy-start | bytes 6148
  33.2 161.6 %reduce-scatter.5.cloned.1.call-start = ((), (), s32[]{:S(2)}) async-start(), calls=%async_computation.3 | async-start | bytes 81920 | tf_op jit(solution)/shard_map/reduce_scatter | solution.py:104
  154.9 17.4 %collective-permute-start.2 = (bf16[2,16,256]{2,1,0:T(8,128)(2,1)S(1)}, bf16[2,16,256]{2,1,0:T(8,128)(2,1)S(1)}, u32[]{:S(2)}, u32[]{:S(2)}) collective-permute-start(bf16[2,16,256]{2,1,0:T(8,128)(2,1)S(1)} %get-tuple-element.13), channel_id=1, source_target_pairs={{4,0},{8,4},{12,8},{5,1},{9,5},{13,9},{6,2},{10,6},{14,10},{7,3},{... | collective-permute-start | bytes 49160 | tf_op jit(solution)/shard_map/ppermute | solution.py:12
  170.9 3.7 %collective-permute-start.3 = (bf16[2,16,256]{2,1,0:T(8,128)(2,1)S(1)}, bf16[2,16,256]{2,1,0:T(8,128)(2,1)S(1)}, u32[]{:S(2)}, u32[]{:S(2)}) collective-permute-start(bf16[2,16,256]{2,1,0:T(8,128)(2,1)S(1)} %copy.171), channel_id=1, source_target_pairs={{0,4},{4,8},{8,12},{1,5},{5,9},{9,13},{2,6},{6,10},{10,14},{3,7},{... | collective-permute-start | bytes 49160 | tf_op jit(solution)/shard_map/ppermute | solution.py:12
Sparse Core Ops, SparseCore 0:
  33.3 21.5 reduce-scatter.2
  174.6 20.1 reduce-scatter.4
where the time goes:
time: 241 us; the launch traced here: 240 us
  blocking collectives  147 us (61%)
  waiting for transfers between devices  41.3 us (17%)
  other arithmetic  16.3 us (7%)
  between operations  15.1 us (6%)
  matrix products  10.7 us (4%)
  starting transfers between devices  5.23 us (2%)
  local copies, waits for them, and re-layouts  4.15 us (2%)
    psum x1, blocking collectives, shards(): norm_now = lax.psum(gram(residual, residual), ('row', 'col'))  57.9 us
    reduce_scatter x2, waiting for transfers between devices, shards(): lax.psum_scatter(row_part.astype(jnp.bfloat16), 'col', scatter_dimension=...  41.3 us
    psum x1, blocking collectives, shards(): norm_next = lax.psum(gram(residual, residual), ('row', 'col'))  30.7 us
    psum x1, blocking collectives, shards(): curv = lax.psum(gram(direction, image), ('row', 'col'))  30.7 us
    all_gather x2, blocking collectives, shards(): row_vec = lax.all_gather(apply_low, 'col', axis=0, tiled=True)  28 us
    another operation x9, other arithmetic, solve_sym(): factor = jnp.linalg.cholesky(sym)  6.4 us
    another operation x6, other arithmetic, solve_sym(): lax.linalg.triangular_solve(factor, inner, left_side=True, lower=True, tr...  5.63 us
    ppermute x4, starting transfers between devices, shifted(): lax.ppermute(value, axis, [(source, source + steps) for source in range(i...  5.15 us
  transfers between devices with their start and end apart: 6, of which 2 were waited for; matrix products, arithmetic and copies ran while one was open for 5% of the time, Pallas kernels for 0%

commit v1 on v0

v1 whole, which is shorter than its diff:
```python
import functools
import jax
import jax.numpy as jnp
from jax import lax
from jax.experimental import pallas as pl
from jax.experimental.pallas import tpu as pltpu
from jax.sharding import PartitionSpec as P

MESH = pl.DeviceIdType.MESH
HIGHEST = lax.Precision.HIGHEST
SEND = jnp.float32


def matmul(a, b, a_dim, b_dim, precision=None):
    return lax.dot_general(
        a,
        b,
        (((a_dim,), (b_dim,)), ((), ())),
        precision=precision,
        preferred_element_type=jnp.float32,
    )


def repeat(count, body):
    if count <= 16:
        for k in range(count):
            body(k)
    else:
        lax.fori_loop(0, count, lambda k, c: (body(k), c)[1], 0)


def eliminate(systems):
    size = systems[0][0].shape[0]
    rows = lax.broadcasted_iota(jnp.int32, (size, 1), 0)
    for k in range(size):
        after = []
        for left, right in systems:
            left_k = left[k : k + 1, :]
            right_k = right[k : k + 1, :]
            inverse = 1.0 / left[k : k + 1, k : k + 1]
            left_k = left_k * inverse
            right_k = right_k * inverse
            factor = left[:, k : k + 1]
            here = rows == k
            after.append(
                (
                    jnp.where(here, left_k, left - factor * left_k),
                    jnp.where(here, right_k, right - factor * right_k),
                )
            )
        systems = after
    return [right for _, right in systems]


def kernel(
    n_row,
    n_col,
    dists,
    probes_hbm,
    mass_hbm,
    blocks_hbm,
    rows_ref,
    cols_ref,
    count_ref,
    solution_ref,
    residual_ref,
    field,
    mass,
    tiles,
    row_field,
    col_field,
    products,
    row_sum,
    row_send,
    col_send,
    row_recv,
    col_recv,
    image,
    gram_send,
    gram_recv,
    in_sem,
    a_send_sem,
    a_recv_sem,
    b_send_sem,
    b_recv_sem,
    g_send_sem,
    g_recv_sem,
):
    row_at = lax.axis_index("row")
    col_at = lax.axis_index("col")
    vb, width, nodes = field.shape
    slots = tiles.shape[0]
    nbr = vb * n_col
    peers = n_row * n_col - 1
    me = row_at * n_col + col_at

    def peer_of(k):
        at = lax.rem(me + k + 1, n_row * n_col)
        return {"row": at // n_col, "col": lax.rem(at, n_col)}

    def col_peer(k):
        return lax.rem(col_at + k, n_col)

    def row_peer(d):
        return lax.rem(row_at + d, n_row)

    loads = [
        pltpu.make_async_copy(probes_hbm, field, in_sem.at[0]),
        pltpu.make_async_copy(mass_hbm, mass, in_sem.at[1]),
    ]
    for s in range(slots):
        loads.append(pltpu.make_async_copy(blocks_hbm.at[0, 0, s], tiles.at[s], in_sem.at[2 + s]))
    for load in loads:
        load.start()

    barrier = pltpu.get_barrier_semaphore()

    def greet(k):
        pl.semaphore_signal(barrier, inc=1, device_id=peer_of(k), device_id_type=MESH)

    repeat(peers, greet)

    live_count = count_ref[0, 0]
    limits, row_of, col_of, row_at_index, col_at_index = [], [], [], [], []
    for s in range(slots):
        live = s < live_count
        lrow = jnp.where(live, rows_ref[0, 0, s], 0)
        lcol = jnp.where(live, cols_ref[0, 0, s], row_at * vb)
        dist = lcol // vb - row_at
        place = jnp.int32(0)
        for at, d in enumerate(dists):
            place = place + jnp.where(dist == d, at, 0)
        part = lax.rem(lcol, vb)
        grow = row_at * nbr + lrow
        gcol = (lcol // vb * n_col + col_at) * vb + part
        limits.append(jnp.where(live, jnp.where(grow == gcol, 0, -nodes), nodes))
        row_of.append(lrow)
        col_of.append(place * vb + part)
        col_at_index.append(place * vb + part)
        row_at_index.append(
            lax.rem(col_at - lrow // vb + n_col, n_col) * vb + lax.rem(lrow, vb)
        )

    def field_to_rows(step):
        to_rows = []
        for at in range(1, len(dists)):
            to_rows.append(
                pltpu.make_async_remote_copy(
                    src_ref=col_field[step].at[pl.ds(0, vb)],
                    dst_ref=col_field[step].at[pl.ds(at * vb, vb)],
                    send_sem=a_send_sem.at[step, at - 1],
                    recv_sem=a_recv_sem.at[step, at - 1],
                    device_id={"row": row_peer(n_row - dists[at]), "col": col_at},
                    device_id_type=MESH,
                )
            )
        return to_rows

    def field_to_cols(step):
        to_cols = []
        for k in range(1, n_col):
            sem = len(dists) - 2 + k
            to_cols.append(
                pltpu.make_async_remote_copy(
                    src_ref=row_field[step].at[pl.ds(0, vb)],
                    dst_ref=row_field[step].at[pl.ds(k * vb, vb)],
                    send_sem=a_send_sem.at[step, sem],
                    recv_sem=a_recv_sem.at[step, sem],
                    device_id={"row": row_at, "col": col_peer(k)},
                    device_id_type=MESH,
                )
            )
        return to_cols

    def parts_to_cols(step):
        to_cols = []
        for k in range(1, n_col):
            to_cols.append(
                pltpu.make_async_remote_copy(
                    src_ref=row_send[step].at[pl.ds(col_peer(k) * vb, vb)],
                    dst_ref=row_recv[step].at[k - 1],
                    send_sem=b_send_sem.at[step, k - 1],
                    recv_sem=b_recv_sem.at[step, k - 1],
                    device_id={"row": row_at, "col": col_peer(k)},
                    device_id_type=MESH,
                )
            )
        return to_cols

    def parts_to_rows(step):
        to_rows = []
        for at in range(1, len(dists)):
            sem = n_col - 2 + at
            to_rows.append(
                pltpu.make_async_remote_copy(
                    src_ref=col_send[step].at[at - 1],
                    dst_ref=col_recv[step].at[at - 1],
                    send_sem=b_send_sem.at[step, sem],
                    recv_sem=b_recv_sem.at[step, sem],
                    device_id={"row": row_peer(dists[at]), "col": col_at},
                    device_id_type=MESH,
                )
            )
        return to_rows

    def gram_copy(step, k):
        return pltpu.make_async_remote_copy(
            src_ref=gram_send[step],
            dst_ref=gram_recv[step].at[k],
            send_sem=g_send_sem.at[step, k],
            recv_sem=g_recv_sem.at[step, k],
            device_id=peer_of(k),
            device_id_type=MESH,
        )

    def publish(step, low):
        row_field[step][0:vb] = low
        col_field[step][0:vb] = low

    def start(copies):
        for copy in copies:
            copy.start()

    def scattered(targets, of):
        sums = []
        for target in range(targets):
            total = jnp.zeros((width, nodes), jnp.float32)
            for s in range(slots):
                total = total + jnp.where(of[s] == target, products[s], 0.0)
            sums.append(total)
        return sums

    def forward(step):
        for copy in field_to_rows(step):
            copy.wait_recv()
        for s in range(slots):
            products[s] = matmul(col_field[step][col_at_index[s]], tiles[s], 1, 1)
        for target, total in enumerate(scattered(nbr, row_of)):
            row_sum[target] = total
            row_send[step][target] = total.astype(SEND)
        start(parts_to_cols(step))

    def backward(step):
        for copy in field_to_cols(step):
            copy.wait_recv()
        for s in range(slots):
            products[s] = matmul(row_field[step][row_at_index[s]], tiles[s], 1, 0)
        sums = scattered(len(dists) * vb, col_of)
        for at in range(1, len(dists)):
            for v in range(vb):
                col_send[step][at - 1, v] = sums[at * vb + v].astype(SEND)
        start(parts_to_rows(step))
        return [sums[v] + row_sum[col_at * vb + v] for v in range(vb)]

    def combined(step, totals):
        for copy in parts_to_cols(step) + parts_to_rows(step):
            copy.wait_recv()
        for k in range(n_col - 1):
            totals = [totals[v] + row_recv[step][k, v].astype(jnp.float32) for v in range(vb)]
        for at in range(len(dists) - 1):
            totals = [totals[v] + col_recv[step][at, v].astype(jnp.float32) for v in range(vb)]
        return totals

    loads[0].wait()
    publish(0, field[...].astype(jnp.bfloat16))
    pl.semaphore_wait(barrier, peers)
    start(field_to_rows(0) + field_to_cols(0))
    ahead = lax.broadcasted_iota(jnp.int32, (nodes, nodes), 1) - lax.broadcasted_iota(
        jnp.int32, (nodes, nodes), 0
    )
    loads[1].wait()
    for s in range(slots):
        loads[2 + s].wait()
        tiles[s] = jnp.where(ahead > limits[s], tiles[s], jnp.zeros_like(tiles[s]))
    forward(0)
    totals = combined(0, backward(0))
    for v in range(vb):
        image[v] = totals[v] + mass[v : v + 1, :] * field[v]

    publish(1, image[...].astype(jnp.bfloat16))
    start(field_to_rows(1) + field_to_cols(1))

    def gram(first, second):
        total = None
        for v in range(vb):
            term = matmul(first[v], second[v], 1, 1, HIGHEST)
            total = term if total is None else total + term
        return total

    gram_send[0][:, 0:width] = gram(field, field)
    gram_send[0][:, width : 2 * width] = gram(field, image)
    gram_send[0][:, 2 * width : 3 * width] = gram(image, field)
    gram_send[0][:, 3 * width : 4 * width] = gram(image, image)
    repeat(peers, lambda k: gram_copy(0, k).start())
    forward(1)
    totals = backward(1)

    def gathered(step):
        repeat(peers, lambda k: gram_copy(step, k).wait_recv())
        total = gram_send[step][...]
        if peers <= 16:
            for k in range(peers):
                total = total + gram_recv[step][k]
            return total
        return lax.fori_loop(0, peers, lambda k, t: t + gram_recv[step][k], total)

    grams = gathered(0)
    norm = grams[:, 0:width]
    curv = grams[:, width : 2 * width]
    curv_t = grams[:, 2 * width : 3 * width]
    square = grams[:, 3 * width : 4 * width]
    unit = (
        lax.broadcasted_iota(jnp.int32, (width, width), 0)
        == lax.broadcasted_iota(jnp.int32, (width, width), 1)
    ).astype(jnp.float32)
    alpha, norm_inverse = eliminate([(0.5 * (curv + curv_t), norm), (norm, unit)])
    norm_next = (
        norm
        - matmul(curv, alpha, 1, 0, HIGHEST)
        - matmul(alpha, curv_t - matmul(square, alpha, 1, 0, HIGHEST), 0, 0, HIGHEST)
    )
    beta = matmul(norm_inverse, norm_next, 1, 0, HIGHEST)
    ahead_mix = unit + beta

    def mix(values, coef):
        return [matmul(coef, values[v], 0, 0, HIGHEST) for v in range(vb)]

    image_alpha = mix(image, alpha)
    field_alpha = mix(field, alpha)
    field_ahead = mix(field, ahead_mix)
    image_ahead = mix(image, ahead_mix)
    direction = [field_ahead[v] - image_alpha[v] for v in range(vb)]
    totals = combined(1, totals)
    second = [totals[v] + mass[v : v + 1, :] * image[v] for v in range(vb)]
    second_alpha = mix(second, alpha)
    image_next = [image_ahead[v] - second_alpha[v] for v in range(vb)]
    gram_send[1][:, 0:width] = 0.5 * (gram(direction, image_next) + gram(image_next, direction))
    repeat(peers, lambda k: gram_copy(1, k).start())
    last = gathered(1)[:, 0:width]
    (alpha_next,) = eliminate([(last, norm_next)])
    direction_alpha = mix(direction, alpha_next)
    image_next_alpha = mix(image_next, alpha_next)
    for v in range(vb):
        solution_ref[v] = field_alpha[v] + direction_alpha[v]
        residual_ref[v] = (field[v] - image_alpha[v]) - image_next_alpha[v]

    for step in range(2):
        for copies in (field_to_rows, field_to_cols, parts_to_cols, parts_to_rows):
            for copy in copies(step):
                copy.wait_send()
        repeat(peers, lambda k: gram_copy(step, k).wait_send())


def shards(probes, mass, blocks, slot_rows, slot_cols, slot_count):
    vb, width, nodes = probes.shape
    n_col = lax.axis_size("col")
    n_row = lax.axis_size("row")
    slots = blocks.shape[2]
    nbr = vb * n_col
    total_blocks = vb * n_col * n_row
    plane = total_blocks // 8
    offsets = [0, 1, 2, plane - 1, plane, plane + 1, 2 * plane]
    deltas = sorted(set([o // vb for o in offsets] + [(o + vb - 1) // vb for o in offsets]))
    dists = sorted(
        set(
            (first + d) // n_col
            for first in range(n_col)
            for d in deltas
            if (first + d) // n_col < n_row
        )
    )
    peers = n_row * n_col - 1
    low = jnp.bfloat16
    f32 = jnp.float32

    def twice(shape, dtype):
        return [pltpu.VMEM(shape, dtype), pltpu.VMEM(shape, dtype)]

    links = len(dists) - 1 + n_col - 1
    smem = pl.BlockSpec(memory_space=pltpu.SMEM)
    hbm = pl.BlockSpec(memory_space=pl.ANY)
    vmem = pl.BlockSpec(memory_space=pltpu.VMEM)
    out = jax.ShapeDtypeStruct((vb, width, nodes), f32)
    return pl.pallas_call(
        functools.partial(kernel, n_row, n_col, dists),
        out_shape=(out, out),
        in_specs=[hbm, hbm, hbm, smem, smem, smem],
        out_specs=(vmem, vmem),
        scratch_shapes=[
            pltpu.VMEM((vb, width, nodes), f32),
            pltpu.VMEM((vb, nodes), f32),
            pltpu.VMEM((slots, nodes, nodes), low),
            twice((nbr, width, nodes), low),
            twice((len(dists) * vb, width, nodes), low),
            pltpu.VMEM((slots, width, nodes), f32),
            pltpu.VMEM((nbr, width, nodes), f32),
            twice((nbr, width, nodes), SEND),
            twice((len(dists) - 1, vb, width, nodes), SEND),
            twice((n_col - 1, vb, width, nodes), SEND),
            twice((len(dists) - 1, vb, width, nodes), SEND),
            pltpu.VMEM((vb, width, nodes), f32),
            twice((width, 128), f32),
            twice((peers, width, 128), f32),
            pltpu.SemaphoreType.DMA((2 + slots,)),
            pltpu.SemaphoreType.DMA((2, links)),
            pltpu.SemaphoreType.DMA((2, links)),
            pltpu.SemaphoreType.DMA((2, links)),
            pltpu.SemaphoreType.DMA((2, links)),
            pltpu.SemaphoreType.DMA((2, peers)),
            pltpu.SemaphoreType.DMA((2, peers)),
        ],
        compiler_params=pltpu.CompilerParams(
            collective_id=0, has_side_effects=True, vmem_limit_bytes=60 * 1024 * 1024
        ),
    )(probes, mass, blocks, slot_rows, slot_cols, slot_count)


def solution(mesh):
    placed = (
        P(("grp", "row", "col"), None, None),
        P(("grp", "row", "col"), None),
        P(("grp", "row"), "col", None, None, None),
        P(("grp", "row"), "col", None),
        P(("grp", "row"), "col", None),
        P(("grp", "row"), "col"),
    )
    return jax.shard_map(
        shards,
        mesh=mesh,
        in_specs=placed,
        out_specs=(P(("grp", "row", "col"), None, None), P(("grp", "row", "col"), None, None)),
        check_vma=False,
    )
```

time: 241 us -> 36.4 us (0.15)
  blocking collectives: 147 us -> 0 us
  waiting for transfers between devices: 41.3 us -> 0 us
  Pallas kernels: 0 us -> 32.1 us
  other arithmetic: 16.3 us -> 0 us
  between operations: 15.1 us -> 1.29 us
  matrix products: 10.7 us -> 0 us
  starting transfers between devices: 5.23 us -> 0 us
    psum x3 -> x0, blocking collectives: 119 us -> none  [the longest x1 57.9 us: shards(): norm_now = lax.psum(gram(residual, residual), ('row', 'col'))]
    reduce_scatter x2 -> x0, waiting for transfers between devices: 41.3 us -> none  [shards(): lax.psum_scatter(row_part.astype(jnp.bfloat16), 'col', scatter_dimension=...]
    pallas_call x0 -> x1, Pallas kernels: none -> 32.1 us  [shards(): pl.pallas_call(functools.partial(kernel, n_row, n_col, dists), out_shape=...]
    all_gather x2 -> x0, blocking collectives: 28 us -> none  [shards(): row_vec = lax.all_gather(apply_low, 'col', axis=0, tiled=True)]
    another operation x18 -> x0, other arithmetic: 12.1 us -> none  [the longest x9 6.4 us: solve_sym(): factor = jnp.linalg.cholesky(sym)]
    dot_general x19 -> x0, matrix products: 9.44 us -> none  [the longest x5 3.51 us: mix(): jnp.einsum('ipk,pq->iqk', field, coef, precision=lax.Precision.HIGHEST)]
    ppermute x4 -> x0, starting transfers between devices: 5.15 us -> none  [shifted(): lax.ppermute(value, axis, [(source, source + steps) for source in range(i...]
    unnamed x8 -> x2, local copies, waits for them, and re-layouts: 0.02 us -> 2.75 us
  transfers between devices with their start and end apart: 6 -> 0, of which waited for: 2 -> 0; matrix products, arithmetic and copies ran while one was open for 5% -> 0% of each run, Pallas kernels for 0% -> 0%
where the time goes in v1:
time: 36.4 us; the launch traced here: 36.1 us
  Pallas kernels  32.1 us (88%)
  local copies, waits for them, and re-layouts  2.75 us (8%)
  between operations  1.29 us (4%)
    pallas_call x1, Pallas kernels, shards(): pl.pallas_call(functools.partial(kernel, n_row, n_col, dists), out_shape=...  32.1 us
    unnamed x2, local copies, waits for them, and re-layouts  2.75 us

profile of v1, /device:TPU:0, one launch (start us, length us, event | category | flops | bytes accessed | tf_op | source)
XLA Modules:
  0.0 36.1 jit_solution(7519320781394075349)
XLA Ops:
  1.3 32.1 %shard_map.77 = (f32[2,16,256]{2,1,0:T(8,128)}, f32[2,16,256]{2,1,0:T(8,128)}) custom-call(f32[2,16,256]{2,1,0:T(8,128)} %probes_hbm.1, f32[2,256]{1,0:T(2,128)} %mass_hbm.1, bf16[1,1,14,256,256]{4,3,2,1,0:T(8,128)(2,1)} %blocks_hbm.1, s32[1,1,14]{2,1,0:T(1,128)} %rows_ref.1, s32[1,1,14]{2,1,0:T(1,128)} %cols_ref.1, s32[1,1]{1,0:T(1,128)S(6)} %copy.10.count_ref), custom_call_target="tpu_custom_call" | custom-call | tf_op jit(solution)/shard_map/pallas_call | solution.py:384
  33.4 1.4 %copy.11 = f32[2,16,256]{2,1,0:T(8,128)} copy(f32[2,16,256]{2,1,0:T(8,128)} %get-tuple-element.4) | data formatting | bytes 65536
  34.8 1.4 %copy.12 = f32[2,16,256]{2,1,0:T(8,128)} copy(f32[2,16,256]{2,1,0:T(8,128)} %get-tuple-element.5) | data formatting | bytes 65536

commit v2 on v1

--- a/solution.py
+++ b/solution.py
@@ -8,7 +8,7 @@
 
 MESH = pl.DeviceIdType.MESH
 HIGHEST = lax.Precision.HIGHEST
-SEND = jnp.float32
+SEND = jnp.bfloat16
 
 
 def matmul(a, b, a_dim, b_dim, precision=None):
@@ -142,64 +142,56 @@
         )
 
     def field_to_rows(step):
-        to_rows = []
+        to_rows = {}
         for at in range(1, len(dists)):
-            to_rows.append(
-                pltpu.make_async_remote_copy(
-                    src_ref=col_field[step].at[pl.ds(0, vb)],
-                    dst_ref=col_field[step].at[pl.ds(at * vb, vb)],
-                    send_sem=a_send_sem.at[step, at - 1],
-                    recv_sem=a_recv_sem.at[step, at - 1],
-                    device_id={"row": row_peer(n_row - dists[at]), "col": col_at},
-                    device_id_type=MESH,
-                )
+            to_rows["fr", step, at] = pltpu.make_async_remote_copy(
+                src_ref=col_field[step].at[pl.ds(0, vb)],
+                dst_ref=col_field[step].at[pl.ds(at * vb, vb)],
+                send_sem=a_send_sem.at[step, at - 1],
+                recv_sem=a_recv_sem.at[step, at - 1],
+                device_id={"row": row_peer(n_row - dists[at]), "col": col_at},
+                device_id_type=MESH,
             )
         return to_rows
 
     def field_to_cols(step):
-        to_cols = []
+        to_cols = {}
         for k in range(1, n_col):
             sem = len(dists) - 2 + k
-            to_cols.append(
-                pltpu.make_async_remote_copy(
-                    src_ref=row_field[step].at[pl.ds(0, vb)],
-                    dst_ref=row_field[step].at[pl.ds(k * vb, vb)],
-                    send_sem=a_send_sem.at[step, sem],
-                    recv_sem=a_recv_sem.at[step, sem],
-                    device_id={"row": row_at, "col": col_peer(k)},
-                    device_id_type=MESH,
-                )
+            to_cols["fc", step, k] = pltpu.make_async_remote_copy(
+                src_ref=row_field[step].at[pl.ds(0, vb)],
+                dst_ref=row_field[step].at[pl.ds(k * vb, vb)],
+                send_sem=a_send_sem.at[step, sem],
+                recv_sem=a_recv_sem.at[step, sem],
+                device_id={"row": row_at, "col": col_peer(k)},
+                device_id_type=MESH,
             )
         return to_cols
 
     def parts_to_cols(step):
-        to_cols = []
+        to_cols = {}
         for k in range(1, n_col):
-            to_cols.append(
-                pltpu.make_async_remote_copy(
-                    src_ref=row_send[step].at[pl.ds(col_peer(k) * vb, vb)],
-                    dst_ref=row_recv[step].at[k - 1],
-                    send_sem=b_send_sem.at[step, k - 1],
-                    recv_sem=b_recv_sem.at[step, k - 1],
-                    device_id={"row": row_at, "col": col_peer(k)},
-                    device_id_type=MESH,
-                )
+            to_cols["pc", step, k] = pltpu.make_async_remote_copy(
+                src_ref=row_send[step].at[pl.ds(col_peer(k) * vb, vb)],
+                dst_ref=row_recv[step].at[k - 1],
+                send_sem=b_send_sem.at[step, k - 1],
+                recv_sem=b_recv_sem.at[step, k - 1],
+                device_id={"row": row_at, "col": col_peer(k)},
+                device_id_type=MESH,
             )
         return to_cols
 
     def parts_to_rows(step):
-        to_rows = []
+        to_rows = {}
         for at in range(1, len(dists)):
             sem = n_col - 2 + at
-            to_rows.append(
-                pltpu.make_async_remote_copy(
-                    src_ref=col_send[step].at[at - 1],
-                    dst_ref=col_recv[step].at[at - 1],
-                    send_sem=b_send_sem.at[step, sem],
-                    recv_sem=b_recv_sem.at[step, sem],
-                    device_id={"row": row_peer(dists[at]), "col": col_at},
-                    device_id_type=MESH,
-                )
+            to_rows["pr", step, at] = pltpu.make_async_remote_copy(
+                src_ref=col_send[step].at[at - 1],
+                dst_ref=col_recv[step].at[at - 1],
+                send_sem=b_send_sem.at[step, sem],
+                recv_sem=b_recv_sem.at[step, sem],
+                device_id={"row": row_peer(dists[at]), "col": col_at},
+                device_id_type=MESH,
             )
         return to_rows
 
@@ -213,13 +205,35 @@
             device_id_type=MESH,
         )
 
-    def publish(step, low):
-        row_field[step][0:vb] = low
-        col_field[step][0:vb] = low
+    def publish(step, values):
+        for v in range(vb):
+            high = values[v].astype(jnp.bfloat16)
+            low = (values[v] - high.astype(jnp.float32)).astype(jnp.bfloat16)
+            for ref in (row_field[step], col_field[step]):
+                ref[v, 0:width] = high
+                ref[v, width : 2 * width] = low
+
+    def product(values, tile, dim):
+        both = matmul(values, tile, 1, dim)
+        return both[0:width] + both[width : 2 * width]
+
+    sent, arrived = {}, set()
 
     def start(copies):
-        for copy in copies:
+        for key, copy in copies.items():
             copy.start()
+            sent[key] = copy
+
+    def arrive(copies):
+        for key, copy in copies.items():
+            copy.wait_recv()
+            arrived.add(key)
+
+    grams_sent, grams_in = [], []
+
+    def start_grams(step):
+        repeat(peers, lambda k: gram_copy(step, k).start())
+        grams_sent.append(step)
 
     def scattered(targets, of):
         sums = []
@@ -231,20 +245,18 @@
         return sums
 
     def forward(step):
-        for copy in field_to_rows(step):
-            copy.wait_recv()
+        arrive(field_to_rows(step))
         for s in range(slots):
-            products[s] = matmul(col_field[step][col_at_index[s]], tiles[s], 1, 1)
+            products[s] = product(col_field[step][col_at_index[s]], tiles[s], 1)
         for target, total in enumerate(scattered(nbr, row_of)):
             row_sum[target] = total
             row_send[step][target] = total.astype(SEND)
         start(parts_to_cols(step))
 
     def backward(step):
-        for copy in field_to_cols(step):
-            copy.wait_recv()
+        arrive(field_to_cols(step))
         for s in range(slots):
-            products[s] = matmul(row_field[step][row_at_index[s]], tiles[s], 1, 0)
+            products[s] = product(row_field[step][row_at_index[s]], tiles[s], 0)
         sums = scattered(len(dists) * vb, col_of)
         for at in range(1, len(dists)):
             for v in range(vb):
@@ -253,18 +265,23 @@
         return [sums[v] + row_sum[col_at * vb + v] for v in range(vb)]
 
     def combined(step, totals):
-        for copy in parts_to_cols(step) + parts_to_rows(step):
-            copy.wait_recv()
+        arrive(parts_to_cols(step) | parts_to_rows(step))
         for k in range(n_col - 1):
             totals = [totals[v] + row_recv[step][k, v].astype(jnp.float32) for v in range(vb)]
         for at in range(len(dists) - 1):
             totals = [totals[v] + col_recv[step][at, v].astype(jnp.float32) for v in range(vb)]
         return totals
 
+    def finish():
+        for copy in sent.values():
+            copy.wait_send()
+        for step in grams_sent:
+            repeat(peers, lambda k: gram_copy(step, k).wait_send())
+
     loads[0].wait()
-    publish(0, field[...].astype(jnp.bfloat16))
+    publish(0, field)
     pl.semaphore_wait(barrier, peers)
-    start(field_to_rows(0) + field_to_cols(0))
+    start(field_to_rows(0) | field_to_cols(0))
     ahead = lax.broadcasted_iota(jnp.int32, (nodes, nodes), 1) - lax.broadcasted_iota(
         jnp.int32, (nodes, nodes), 0
     )
@@ -277,8 +294,8 @@
     for v in range(vb):
         image[v] = totals[v] + mass[v : v + 1, :] * field[v]
 
-    publish(1, image[...].astype(jnp.bfloat16))
-    start(field_to_rows(1) + field_to_cols(1))
+    publish(1, image)
+    start(field_to_rows(1) | field_to_cols(1))
 
     def gram(first, second):
         total = None
@@ -291,11 +308,12 @@
     gram_send[0][:, width : 2 * width] = gram(field, image)
     gram_send[0][:, 2 * width : 3 * width] = gram(image, field)
     gram_send[0][:, 3 * width : 4 * width] = gram(image, image)
-    repeat(peers, lambda k: gram_copy(0, k).start())
+    start_grams(0)
     forward(1)
     totals = backward(1)
 
     def gathered(step):
+        grams_in.append(step)
         repeat(peers, lambda k: gram_copy(step, k).wait_recv())
         total = gram_send[step][...]
         if peers <= 16:
@@ -335,7 +353,7 @@
     second_alpha = mix(second, alpha)
     image_next = [image_ahead[v] - second_alpha[v] for v in range(vb)]
     gram_send[1][:, 0:width] = 0.5 * (gram(direction, image_next) + gram(image_next, direction))
-    repeat(peers, lambda k: gram_copy(1, k).start())
+    start_grams(1)
     last = gathered(1)[:, 0:width]
     (alpha_next,) = eliminate([(last, norm_next)])
     direction_alpha = mix(direction, alpha_next)
@@ -344,11 +362,7 @@
         solution_ref[v] = field_alpha[v] + direction_alpha[v]
         residual_ref[v] = (field[v] - image_alpha[v]) - image_next_alpha[v]
 
-    for step in range(2):
-        for copies in (field_to_rows, field_to_cols, parts_to_cols, parts_to_rows):
-            for copy in copies(step):
-                copy.wait_send()
-        repeat(peers, lambda k: gram_copy(step, k).wait_send())
+    finish()
 
 
 def shards(probes, mass, blocks, slot_rows, slot_cols, slot_count):
@@ -390,8 +404,8 @@
             pltpu.VMEM((vb, width, nodes), f32),
             pltpu.VMEM((vb, nodes), f32),
             pltpu.VMEM((slots, nodes, nodes), low),
-            twice((nbr, width, nodes), low),
-            twice((len(dists) * vb, width, nodes), low),
+            twice((nbr, 2 * width, nodes), low),
+            twice((len(dists) * vb, 2 * width, nodes), low),
             pltpu.VMEM((slots, width, nodes), f32),
             pltpu.VMEM((nbr, width, nodes), f32),
             twice((nbr, width, nodes), SEND),

time: 36.4 us -> 37.5 us (1.030)
  Pallas kernels: 32.1 us -> 33.2 us
    pallas_call x1, Pallas kernels: 32.1 us -> 33.2 us  [shards(): pl.pallas_call(functools.partial(kernel, n_row, n_col, dists), out_shape=...]
where the time goes in v2:
time: 37.5 us; the launch traced here: 37.2 us
  Pallas kernels  33.2 us (89%)
  local copies, waits for them, and re-layouts  2.75 us (7%)
  between operations  1.29 us (3%)
    pallas_call x1, Pallas kernels, shards(): pl.pallas_call(functools.partial(kernel, n_row, n_col, dists), out_shape=...  33.2 us
    unnamed x2, local copies, waits for them, and re-layouts  2.75 us

profile of v2, /device:TPU:0, one launch (start us, length us, event | category | flops | bytes accessed | tf_op | source)
XLA Modules:
  0.0 37.2 jit_solution(17277778093182937022)
XLA Ops:
  1.3 33.2 %shard_map.77 = (f32[2,16,256]{2,1,0:T(8,128)}, f32[2,16,256]{2,1,0:T(8,128)}) custom-call(f32[2,16,256]{2,1,0:T(8,128)} %probes_hbm.1, f32[2,256]{1,0:T(2,128)} %mass_hbm.1, bf16[1,1,14,256,256]{4,3,2,1,0:T(8,128)(2,1)} %blocks_hbm.1, s32[1,1,14]{2,1,0:T(1,128)} %rows_ref.1, s32[1,1,14]{2,1,0:T(1,128)} %cols_ref.1, s32[1,1]{1,0:T(1,128)S(6)} %copy.10.count_ref), custom_call_target="tpu_custom_call" | custom-call | tf_op jit(solution)/shard_map/pallas_call | solution.py:398
  34.5 1.4 %copy.11 = f32[2,16,256]{2,1,0:T(8,128)} copy(f32[2,16,256]{2,1,0:T(8,128)} %get-tuple-element.4) | data formatting | bytes 65536
  35.8 1.4 %copy.12 = f32[2,16,256]{2,1,0:T(8,128)} copy(f32[2,16,256]{2,1,0:T(8,128)} %get-tuple-element.5) | data formatting | bytes 65536

commit v3 on v2

--- a/solution.py
+++ b/solution.py
@@ -115,10 +115,10 @@
 
     barrier = pltpu.get_barrier_semaphore()
 
-    def greet(k):
-        pl.semaphore_signal(barrier, inc=1, device_id=peer_of(k), device_id_type=MESH)
-
-    repeat(peers, greet)
+    near = [{"row": row_peer(k), "col": col_at} for k in range(1, n_row)]
+    near += [{"row": row_at, "col": col_peer(k)} for k in range(1, n_col)]
+    for peer in near:
+        pl.semaphore_signal(barrier, inc=1, device_id=peer, device_id_type=MESH)
 
     live_count = count_ref[0, 0]
     limits, row_of, col_of, row_at_index, col_at_index = [], [], [], [], []
@@ -280,8 +280,6 @@
 
     loads[0].wait()
     publish(0, field)
-    pl.semaphore_wait(barrier, peers)
-    start(field_to_rows(0) | field_to_cols(0))
     ahead = lax.broadcasted_iota(jnp.int32, (nodes, nodes), 1) - lax.broadcasted_iota(
         jnp.int32, (nodes, nodes), 0
     )
@@ -289,6 +287,8 @@
     for s in range(slots):
         loads[2 + s].wait()
         tiles[s] = jnp.where(ahead > limits[s], tiles[s], jnp.zeros_like(tiles[s]))
+    pl.semaphore_wait(barrier, len(near))
+    start(field_to_rows(0) | field_to_cols(0))
     forward(0)
     totals = combined(0, backward(0))
     for v in range(vb):
@@ -300,14 +300,25 @@
     def gram(first, second):
         total = None
         for v in range(vb):
-            term = matmul(first[v], second[v], 1, 1, HIGHEST)
+            both = jnp.concatenate([first[v], second[v]], axis=0)
+            term = matmul(both, both, 1, 1, HIGHEST)
             total = term if total is None else total + term
         return total
 
-    gram_send[0][:, 0:width] = gram(field, field)
-    gram_send[0][:, width : 2 * width] = gram(field, image)
-    gram_send[0][:, 2 * width : 3 * width] = gram(image, field)
-    gram_send[0][:, 3 * width : 4 * width] = gram(image, image)
+    groups = 2 * width // 8
+
+    def pack(step, total):
+        for g in range(groups):
+            gram_send[step][:, 2 * width * g : 2 * width * (g + 1)] = total[8 * g : 8 * (g + 1)]
+
+    def unpack(packed):
+        total = jnp.concatenate(
+            [packed[:, 2 * width * g : 2 * width * (g + 1)] for g in range(groups)], axis=0
+        )
+        upper, lower = total[0:width], total[width : 2 * width]
+        return upper[:, 0:width], upper[:, width:], lower[:, 0:width], lower[:, width:]
+
+    pack(0, gram(field, image))
     start_grams(0)
     forward(1)
     totals = backward(1)
@@ -323,10 +334,7 @@
         return lax.fori_loop(0, peers, lambda k, t: t + gram_recv[step][k], total)
 
     grams = gathered(0)
-    norm = grams[:, 0:width]
-    curv = grams[:, width : 2 * width]
-    curv_t = grams[:, 2 * width : 3 * width]
-    square = grams[:, 3 * width : 4 * width]
+    norm, curv, curv_t, square = unpack(grams)
     unit = (
         lax.broadcasted_iota(jnp.int32, (width, width), 0)
         == lax.broadcasted_iota(jnp.int32, (width, width), 1)
@@ -348,14 +356,21 @@
     field_ahead = mix(field, ahead_mix)
     image_ahead = mix(image, ahead_mix)
     direction = [field_ahead[v] - image_alpha[v] for v in range(vb)]
+    known = gram(direction, image_ahead)
+    known_turned = jnp.concatenate([known[:, width:], known[:, 0:width]], axis=1)
     totals = combined(1, totals)
     second = [totals[v] + mass[v : v + 1, :] * image[v] for v in range(vb)]
+    fresh = gram(direction, second)
+    first_half = lax.broadcasted_iota(jnp.int32, (2 * width, 2 * width), 0) < width
+    left_half = lax.broadcasted_iota(jnp.int32, (2 * width, 2 * width), 1) < width
+    pack(1, jnp.where(first_half == left_half, known_turned, fresh))
+    start_grams(1)
     second_alpha = mix(second, alpha)
     image_next = [image_ahead[v] - second_alpha[v] for v in range(vb)]
-    gram_send[1][:, 0:width] = 0.5 * (gram(direction, image_next) + gram(image_next, direction))
-    start_grams(1)
-    last = gathered(1)[:, 0:width]
-    (alpha_next,) = eliminate([(last, norm_next)])
+    known_sum, fresh_sum, fresh_sum_t, known_sum_t = unpack(gathered(1))
+    last = known_sum - matmul(fresh_sum, alpha, 1, 0, HIGHEST)
+    last_t = known_sum_t - matmul(alpha, fresh_sum_t, 0, 0, HIGHEST)
+    (alpha_next,) = eliminate([(0.5 * (last + last_t), norm_next)])
     direction_alpha = mix(direction, alpha_next)
     image_next_alpha = mix(image_next, alpha_next)
     for v in range(vb):
@@ -413,8 +428,8 @@
             twice((n_col - 1, vb, width, nodes), SEND),
             twice((len(dists) - 1, vb, width, nodes), SEND),
             pltpu.VMEM((vb, width, nodes), f32),
-            twice((width, 128), f32),
-            twice((peers, width, 128), f32),
+            twice((8, 4 * width * width // 8), f32),
+            twice((peers, 8, 4 * width * width // 8), f32),
             pltpu.SemaphoreType.DMA((2 + slots,)),
             pltpu.SemaphoreType.DMA((2, links)),
             pltpu.SemaphoreType.DMA((2, links)),

time: 37.5 us -> 34.6 us (0.923)
  Pallas kernels: 33.2 us -> 30.2 us
    pallas_call x1, Pallas kernels: 33.2 us -> 30.2 us  [shards(): pl.pallas_call(functools.partial(kernel, n_row, n_col, dists), out_shape=...]
where the time goes in v3:
time: 34.6 us; the launch traced here: 34.3 us
  Pallas kernels  30.2 us (87%)
  local copies, waits for them, and re-layouts  2.75 us (8%)
  between operations  1.29 us (4%)
    pallas_call x1, Pallas kernels, shards(): pl.pallas_call(functools.partial(kernel, n_row, n_col, dists), out_shape=...  30.2 us
    unnamed x2, local copies, waits for them, and re-layouts  2.75 us

profile of v3, /device:TPU:0, one launch (start us, length us, event | category | flops | bytes accessed | tf_op | source)
XLA Modules:
  0.0 34.3 jit_solution(10870894450814159121)
XLA Ops:
  1.3 30.2 %shard_map.77 = (f32[2,16,256]{2,1,0:T(8,128)}, f32[2,16,256]{2,1,0:T(8,128)}) custom-call(f32[2,16,256]{2,1,0:T(8,128)} %probes_hbm.1, f32[2,256]{1,0:T(2,128)} %mass_hbm.1, bf16[1,1,14,256,256]{4,3,2,1,0:T(8,128)(2,1)} %blocks_hbm.1, s32[1,1,14]{2,1,0:T(1,128)} %rows_ref.1, s32[1,1,14]{2,1,0:T(1,128)} %cols_ref.1, s32[1,1]{1,0:T(1,128)S(6)} %copy.10.count_ref), custom_call_target="tpu_custom_call" | custom-call | tf_op jit(solution)/shard_map/pallas_call | solution.py:413
  31.5 1.4 %copy.11 = f32[2,16,256]{2,1,0:T(8,128)} copy(f32[2,16,256]{2,1,0:T(8,128)} %get-tuple-element.4) | data formatting | bytes 65536
  32.9 1.4 %copy.12 = f32[2,16,256]{2,1,0:T(8,128)} copy(f32[2,16,256]{2,1,0:T(8,128)} %get-tuple-element.5) | data formatting | bytes 65536

commit v4 on v3

--- a/solution.py
+++ b/solution.py
@@ -319,9 +319,24 @@
         return upper[:, 0:width], upper[:, width:], lower[:, 0:width], lower[:, width:]
 
     pack(0, gram(field, image))
+    forward(1)
     start_grams(0)
-    forward(1)
     totals = backward(1)
+    totals = combined(1, totals)
+    second = [totals[v] + mass[v : v + 1, :] * image[v] for v in range(vb)]
+    tall, wide = None, None
+    for v in range(vb):
+        both = jnp.concatenate([field[v], image[v]], axis=0)
+        down = matmul(both, second[v], 1, 1, HIGHEST)
+        across = matmul(second[v], both, 1, 1, HIGHEST)
+        tall = down if tall is None else tall + down
+        wide = across if wide is None else wide + across
+    for g in range(groups):
+        gram_send[1][:, width * g : width * (g + 1)] = tall[8 * g : 8 * (g + 1)]
+    for g in range(groups // 2):
+        at = groups * width + 2 * width * g
+        gram_send[1][:, at : at + 2 * width] = wide[8 * g : 8 * (g + 1)]
+    start_grams(1)
 
     def gathered(step):
         grams_in.append(step)
@@ -356,20 +371,30 @@
     field_ahead = mix(field, ahead_mix)
     image_ahead = mix(image, ahead_mix)
     direction = [field_ahead[v] - image_alpha[v] for v in range(vb)]
-    known = gram(direction, image_ahead)
-    known_turned = jnp.concatenate([known[:, width:], known[:, 0:width]], axis=1)
-    totals = combined(1, totals)
-    second = [totals[v] + mass[v : v + 1, :] * image[v] for v in range(vb)]
-    fresh = gram(direction, second)
-    first_half = lax.broadcasted_iota(jnp.int32, (2 * width, 2 * width), 0) < width
-    left_half = lax.broadcasted_iota(jnp.int32, (2 * width, 2 * width), 1) < width
-    pack(1, jnp.where(first_half == left_half, known_turned, fresh))
-    start_grams(1)
     second_alpha = mix(second, alpha)
     image_next = [image_ahead[v] - second_alpha[v] for v in range(vb)]
-    known_sum, fresh_sum, fresh_sum_t, known_sum_t = unpack(gathered(1))
-    last = known_sum - matmul(fresh_sum, alpha, 1, 0, HIGHEST)
-    last_t = known_sum_t - matmul(alpha, fresh_sum_t, 0, 0, HIGHEST)
+    direction_image = matmul(ahead_mix, curv, 0, 0, HIGHEST) - matmul(
+        alpha, square, 0, 0, HIGHEST
+    )
+    image_direction = matmul(curv_t, ahead_mix, 1, 0, HIGHEST) - matmul(
+        square, alpha, 1, 0, HIGHEST
+    )
+    known = matmul(direction_image, ahead_mix, 1, 0, HIGHEST)
+    known_t = matmul(ahead_mix, image_direction, 0, 0, HIGHEST)
+    weights = jnp.concatenate([ahead_mix, -alpha], axis=0)
+    packed = gathered(1)
+    tall = jnp.concatenate(
+        [packed[:, width * g : width * (g + 1)] for g in range(groups)], axis=0
+    )
+    wide = jnp.concatenate(
+        [
+            packed[:, groups * width + 2 * width * g : groups * width + 2 * width * (g + 1)]
+            for g in range(groups // 2)
+        ],
+        axis=0,
+    )
+    last = known - matmul(matmul(weights, tall, 0, 0, HIGHEST), alpha, 1, 0, HIGHEST)
+    last_t = known_t - matmul(alpha, matmul(wide, weights, 1, 0, HIGHEST), 0, 0, HIGHEST)
     (alpha_next,) = eliminate([(0.5 * (last + last_t), norm_next)])
     direction_alpha = mix(direction, alpha_next)
     image_next_alpha = mix(image_next, alpha_next)
@@ -407,7 +432,7 @@
 
     links = len(dists) - 1 + n_col - 1
     smem = pl.BlockSpec(memory_space=pltpu.SMEM)
-    hbm = pl.BlockSpec(memory_space=pl.ANY)
+    hbm = pl.BlockSpec(memory_space=pltpu.HBM)
     vmem = pl.BlockSpec(memory_space=pltpu.VMEM)
     out = jax.ShapeDtypeStruct((vb, width, nodes), f32)
     return pl.pallas_call(
@@ -439,7 +464,7 @@
             pltpu.SemaphoreType.DMA((2, peers)),
         ],
         compiler_params=pltpu.CompilerParams(
-            collective_id=0, has_side_effects=True, vmem_limit_bytes=60 * 1024 * 1024
+            collective_id=0, has_side_effects=True, vmem_limit_bytes=32 * 1024 * 1024
         ),
     )(probes, mass, blocks, slot_rows, slot_cols, slot_count)
 

time: 34.6 us -> 35.9 us (1.038)
  local copies, waits for them, and re-layouts: 2.75 us -> 5.47 us
  Pallas kernels: 30.2 us -> 28.9 us
    unnamed x2 -> x12, local copies, waits for them, and re-layouts: 2.75 us -> 5.47 us
    pallas_call x1, Pallas kernels: 30.2 us -> 28.9 us  [shards(): pl.pallas_call(functools.partial(kernel, n_row, n_col, dists), out_shape=...]
where the time goes in v4:
time: 35.9 us; the launch traced here: 35.7 us
  Pallas kernels  28.9 us (81%)
  local copies, waits for them, and re-layouts  5.47 us (15%)
  between operations  1.3 us (4%)
    pallas_call x1, Pallas kernels, shards(): pl.pallas_call(functools.partial(kernel, n_row, n_col, dists), out_shape=...  28.9 us
    unnamed x12, local copies, waits for them, and re-layouts  5.47 us

profile of v4, /device:TPU:0, one launch (start us, length us, event | category | flops | bytes accessed | tf_op | source)
XLA Modules:
  0.0 35.7 jit_solution(13763049082074321775)
XLA Ops:
  1.3 0.0 copy-start
  1.3 1.5 %copy-done = bf16[1,1,14,256,256]{4,3,2,1,0:T(8,128)(2,1)S(1)} copy-done((bf16[1,1,14,256,256]{4,3,2,1,0:T(8,128)(2,1)S(1)}, bf16[1,1,14,256,256]{4,3,2,1,0:T(8,128)(2,1)}, u32[]{:S(2)}) %copy-start) | copy-done | bytes 1835032
  2.8 0.0 copy-start.1
  2.8 0.8 %copy-done.1 = f32[2,16,256]{2,1,0:T(8,128)S(1)} copy-done((f32[2,16,256]{2,1,0:T(8,128)S(1)}, f32[2,16,256]{2,1,0:T(8,128)}, u32[]{:S(2)}) %copy-start.1) | copy-done | bytes 32792
  3.5 0.0 copy-start.2
  3.5 0.7 %copy-done.2 = f32[2,256]{1,0:T(2,128)S(1)} copy-done((f32[2,256]{1,0:T(2,128)S(1)}, f32[2,256]{1,0:T(2,128)}, u32[]{:S(2)}) %copy-start.2) | copy-done | bytes 2072
  4.2 0.0 copy-start.3
  4.2 0.7 %copy-done.3 = s32[1,1,14]{2,1,0:T(1,128)S(1)} copy-done((s32[1,1,14]{2,1,0:T(1,128)S(1)}, s32[1,1,14]{2,1,0:T(1,128)}, u32[]{:S(2)}) %copy-start.3) | copy-done | bytes 80
  4.9 0.0 copy-start.4
  4.9 0.7 %copy-done.4 = s32[1,1,14]{2,1,0:T(1,128)S(1)} copy-done((s32[1,1,14]{2,1,0:T(1,128)S(1)}, s32[1,1,14]{2,1,0:T(1,128)}, u32[]{:S(2)}) %copy-start.4) | copy-done | bytes 80
  5.5 28.9 %shard_map.77 = (f32[2,16,256]{2,1,0:T(8,128)S(1)}, f32[2,16,256]{2,1,0:T(8,128)S(1)}) custom-call(f32[2,16,256]{2,1,0:T(8,128)S(1)} %copy-done.1, f32[2,256]{1,0:T(2,128)S(1)} %copy-done.2, bf16[1,1,14,256,256]{4,3,2,1,0:T(8,128)(2,1)S(1)} %copy-done, s32[1,1,14]{2,1,0:T(1,128)S(1)} %copy-done.3, s32[1,1,14]{2,1,0:T(1,128)S(1)} %copy-done.4, ...), custom_call_target="tpu_custom_call" | custom-call | tf_op jit(solution)/shard_map/pallas_call | solution.py:438
  34.4 0.6 %copy.11 = f32[2,16,256]{2,1,0:T(8,128)} copy(f32[2,16,256]{2,1,0:T(8,128)S(1)} %get-tuple-element.4) | data formatting | bytes 65536
  35.1 0.6 %copy.12 = f32[2,16,256]{2,1,0:T(8,128)} copy(f32[2,16,256]{2,1,0:T(8,128)S(1)} %get-tuple-element.5) | data formatting | bytes 65536
Async XLA Ops:
  1.3 1.5 %copy-start = (bf16[1,1,14,256,256]{4,3,2,1,0:T(8,128)(2,1)S(1)}, bf16[1,1,14,256,256]{4,3,2,1,0:T(8,128)(2,1)}, u32[]{:S(2)}) copy-start(bf16[1,1,14,256,256]{4,3,2,1,0:T(8,128)(2,1)} %blocks_hbm.1) | copy-start | bytes 5505028
  2.8 0.8 %copy-start.1 = (f32[2,16,256]{2,1,0:T(8,128)S(1)}, f32[2,16,256]{2,1,0:T(8,128)}, u32[]{:S(2)}) copy-start(f32[2,16,256]{2,1,0:T(8,128)} %probes_hbm.1) | copy-start | bytes 98308
  3.5 0.7 %copy-start.2 = (f32[2,256]{1,0:T(2,128)S(1)}, f32[2,256]{1,0:T(2,128)}, u32[]{:S(2)}) copy-start(f32[2,256]{1,0:T(2,128)} %mass_hbm.1) | copy-start | bytes 6148
  4.2 0.7 %copy-start.3 = (s32[1,1,14]{2,1,0:T(1,128)S(1)}, s32[1,1,14]{2,1,0:T(1,128)}, u32[]{:S(2)}) copy-start(s32[1,1,14]{2,1,0:T(1,128)} %rows_ref.1) | copy-start | bytes 172
  4.9 0.7 %copy-start.4 = (s32[1,1,14]{2,1,0:T(1,128)S(1)}, s32[1,1,14]{2,1,0:T(1,128)}, u32[]{:S(2)}) copy-start(s32[1,1,14]{2,1,0:T(1,128)} %cols_ref.1) | copy-start | bytes 172

commit v5 on v4

--- a/solution.py
+++ b/solution.py
@@ -432,7 +432,7 @@
 
     links = len(dists) - 1 + n_col - 1
     smem = pl.BlockSpec(memory_space=pltpu.SMEM)
-    hbm = pl.BlockSpec(memory_space=pltpu.HBM)
+    hbm = pl.BlockSpec(memory_space=pl.ANY)
     vmem = pl.BlockSpec(memory_space=pltpu.VMEM)
     out = jax.ShapeDtypeStruct((vb, width, nodes), f32)
     return pl.pallas_call(
@@ -464,7 +464,7 @@
             pltpu.SemaphoreType.DMA((2, peers)),
         ],
         compiler_params=pltpu.CompilerParams(
-            collective_id=0, has_side_effects=True, vmem_limit_bytes=32 * 1024 * 1024
+            collective_id=0, has_side_effects=True, vmem_limit_bytes=57 * 1024 * 1024
         ),
     )(probes, mass, blocks, slot_rows, slot_cols, slot_count)
 

time: 35.9 us -> 31.6 us (0.88)
  local copies, waits for them, and re-layouts: 5.47 us -> 2.75 us
  Pallas kernels: 28.9 us -> 27.3 us
    unnamed x12 -> x2, local copies, waits for them, and re-layouts: 5.47 us -> 2.75 us
    pallas_call x1, Pallas kernels: 28.9 us -> 27.3 us  [shards(): pl.pallas_call(functools.partial(kernel, n_row, n_col, dists), out_shape=...]
where the time goes in v5:
time: 31.6 us; the launch traced here: 31.3 us
  Pallas kernels  27.3 us (86%)
  local copies, waits for them, and re-layouts  2.75 us (9%)
  between operations  1.29 us (4%)
    pallas_call x1, Pallas kernels, shards(): pl.pallas_call(functools.partial(kernel, n_row, n_col, dists), out_shape=...  27.3 us
    unnamed x2, local copies, waits for them, and re-layouts  2.75 us

profile of v5, /device:TPU:0, one launch (start us, length us, event | category | flops | bytes accessed | tf_op | source)
XLA Modules:
  0.0 31.3 jit_solution(10738606090822355235)
XLA Ops:
  1.3 27.3 %shard_map.77 = (f32[2,16,256]{2,1,0:T(8,128)}, f32[2,16,256]{2,1,0:T(8,128)}) custom-call(f32[2,16,256]{2,1,0:T(8,128)} %probes_hbm.1, f32[2,256]{1,0:T(2,128)} %mass_hbm.1, bf16[1,1,14,256,256]{4,3,2,1,0:T(8,128)(2,1)} %blocks_hbm.1, s32[1,1,14]{2,1,0:T(1,128)} %rows_ref.1, s32[1,1,14]{2,1,0:T(1,128)} %cols_ref.1, s32[1,1]{1,0:T(1,128)S(6)} %copy.10.count_ref), custom_call_target="tpu_custom_call" | custom-call | tf_op jit(solution)/shard_map/pallas_call | solution.py:438
  28.6 1.4 %copy.11 = f32[2,16,256]{2,1,0:T(8,128)} copy(f32[2,16,256]{2,1,0:T(8,128)} %get-tuple-element.4) | data formatting | bytes 65536
  29.9 1.4 %copy.12 = f32[2,16,256]{2,1,0:T(8,128)} copy(f32[2,16,256]{2,1,0:T(8,128)} %get-tuple-element.5) | data formatting | bytes 65536

commit v6 on v5

--- a/solution.py
+++ b/solution.py
@@ -62,8 +62,7 @@
     rows_ref,
     cols_ref,
     count_ref,
-    solution_ref,
-    residual_ref,
+    result_ref,
     field,
     mass,
     tiles,
@@ -280,6 +279,8 @@
 
     loads[0].wait()
     publish(0, field)
+    pl.semaphore_wait(barrier, len(near))
+    start(field_to_rows(0) | field_to_cols(0))
     ahead = lax.broadcasted_iota(jnp.int32, (nodes, nodes), 1) - lax.broadcasted_iota(
         jnp.int32, (nodes, nodes), 0
     )
@@ -287,8 +288,6 @@
     for s in range(slots):
         loads[2 + s].wait()
         tiles[s] = jnp.where(ahead > limits[s], tiles[s], jnp.zeros_like(tiles[s]))
-    pl.semaphore_wait(barrier, len(near))
-    start(field_to_rows(0) | field_to_cols(0))
     forward(0)
     totals = combined(0, backward(0))
     for v in range(vb):
@@ -399,8 +398,8 @@
     direction_alpha = mix(direction, alpha_next)
     image_next_alpha = mix(image_next, alpha_next)
     for v in range(vb):
-        solution_ref[v] = field_alpha[v] + direction_alpha[v]
-        residual_ref[v] = (field[v] - image_alpha[v]) - image_next_alpha[v]
+        result_ref[0, v] = field_alpha[v] + direction_alpha[v]
+        result_ref[1, v] = (field[v] - image_alpha[v]) - image_next_alpha[v]
 
     finish()
 
@@ -435,11 +434,11 @@
     hbm = pl.BlockSpec(memory_space=pl.ANY)
     vmem = pl.BlockSpec(memory_space=pltpu.VMEM)
     out = jax.ShapeDtypeStruct((vb, width, nodes), f32)
-    return pl.pallas_call(
+    both = pl.pallas_call(
         functools.partial(kernel, n_row, n_col, dists),
-        out_shape=(out, out),
+        out_shape=jax.ShapeDtypeStruct((2, vb, width, nodes), f32),
         in_specs=[hbm, hbm, hbm, smem, smem, smem],
-        out_specs=(vmem, vmem),
+        out_specs=vmem,
         scratch_shapes=[
             pltpu.VMEM((vb, width, nodes), f32),
             pltpu.VMEM((vb, nodes), f32),
@@ -467,6 +466,7 @@
             collective_id=0, has_side_effects=True, vmem_limit_bytes=57 * 1024 * 1024
         ),
     )(probes, mass, blocks, slot_rows, slot_cols, slot_count)
+    return both[0], both[1]
 
 
 def solution(mesh):

time: 31.6 us -> 30.1 us (0.953)
  local copies, waits for them, and re-layouts: 2.75 us -> 1.41 us
    unnamed x2 -> x0, local copies, waits for them, and re-layouts: 2.75 us -> none
    squeeze x0 -> x1, local copies, waits for them, and re-layouts: none -> 1.41 us  [shards(): return (both[0], both[1])]
where the time goes in v6:
time: 30.1 us; the launch traced here: 29.9 us
  Pallas kernels  27.2 us (90%)
  local copies, waits for them, and re-layouts  1.41 us (5%)
  between operations  1.29 us (4%)
    pallas_call x1, Pallas kernels, shards(): pl.pallas_call(functools.partial(kernel, n_row, n_col, dists), out_shape=...  27.2 us
    squeeze x1, local copies, waits for them, and re-layouts, shards(): return (both[0], both[1])  1.41 us

profile of v6, /device:TPU:0, one launch (start us, length us, event | category | flops | bytes accessed | tf_op | source)
XLA Modules:
  0.0 29.9 jit_solution(3598151327444538182)
XLA Ops:
  1.3 27.2 %shard_map.77 = f32[2,2,16,256]{3,2,1,0:T(8,128)} custom-call(f32[2,16,256]{2,1,0:T(8,128)} %probes_hbm.1, f32[2,256]{1,0:T(2,128)} %mass_hbm.1, bf16[1,1,14,256,256]{4,3,2,1,0:T(8,128)(2,1)} %blocks_hbm.1, s32[1,1,14]{2,1,0:T(1,128)} %rows_ref.1, s32[1,1,14]{2,1,0:T(1,128)} %cols_ref.1, s32[1,1]{1,0:T(1,128)S(6)} %copy.8.count_ref), custom_call_target="tpu_custom_call" | custom-call | tf_op jit(solution)/shard_map/pallas_call | solution.py:437
  28.5 1.4 %slice_bitcast_fusion = (f32[2,16,256]{2,1,0:T(8,128)}, f32[2,16,256]{2,1,0:T(8,128)}) fusion(f32[2,2,16,256]{3,2,1,0:T(8,128)} %shard_map.77), kind=kLoop, calls=%fused_computation | loop fusion | bytes 131072 | tf_op jit(solution)/shard_map/squeeze | solution.py:469

commit v7 on v6

--- a/solution.py
+++ b/solution.py
@@ -381,6 +381,7 @@
     known = matmul(direction_image, ahead_mix, 1, 0, HIGHEST)
     known_t = matmul(ahead_mix, image_direction, 0, 0, HIGHEST)
     weights = jnp.concatenate([ahead_mix, -alpha], axis=0)
+    finish()
     packed = gathered(1)
     tall = jnp.concatenate(
         [packed[:, width * g : width * (g + 1)] for g in range(groups)], axis=0
@@ -400,8 +401,6 @@
     for v in range(vb):
         result_ref[0, v] = field_alpha[v] + direction_alpha[v]
         result_ref[1, v] = (field[v] - image_alpha[v]) - image_next_alpha[v]
-
-    finish()
 
 
 def shards(probes, mass, blocks, slot_rows, slot_cols, slot_count):

time: 30.1 us -> 30 us (level)
  no operation moved by 1% of the time
where the time goes in v7:
time: 30 us; the launch traced here: 29.8 us
  Pallas kernels  27.1 us (90%)
  local copies, waits for them, and re-layouts  1.41 us (5%)
  between operations  1.29 us (4%)
    pallas_call x1, Pallas kernels, shards(): pl.pallas_call(functools.partial(kernel, n_row, n_col, dists), out_shape=...  27.1 us
    squeeze x1, local copies, waits for them, and re-layouts, shards(): return (both[0], both[1])  1.41 us

profile of v7, /device:TPU:0, one launch (start us, length us, event | category | flops | bytes accessed | tf_op | source)
XLA Modules:
  0.0 29.8 jit_solution(5905628145261488073)
XLA Ops:
  1.3 27.1 %shard_map.77 = f32[2,2,16,256]{3,2,1,0:T(8,128)} custom-call(f32[2,16,256]{2,1,0:T(8,128)} %probes_hbm.1, f32[2,256]{1,0:T(2,128)} %mass_hbm.1, bf16[1,1,14,256,256]{4,3,2,1,0:T(8,128)(2,1)} %blocks_hbm.1, s32[1,1,14]{2,1,0:T(1,128)} %rows_ref.1, s32[1,1,14]{2,1,0:T(1,128)} %cols_ref.1, s32[1,1]{1,0:T(1,128)S(6)} %copy.8.count_ref), custom_call_target="tpu_custom_call" | custom-call | tf_op jit(solution)/shard_map/pallas_call | solution.py:436
  28.4 1.4 %slice_bitcast_fusion = (f32[2,16,256]{2,1,0:T(8,128)}, f32[2,16,256]{2,1,0:T(8,128)}) fusion(f32[2,2,16,256]{3,2,1,0:T(8,128)} %shard_map.77), kind=kLoop, calls=%fused_computation | loop fusion | bytes 131072 | tf_op jit(solution)/shard_map/squeeze | solution.py:468
